TPU v7x, 128 devices: a whole 4x4x4 slice. The times are simulated.
128 devices in a mesh: rep: 16 (over x, z), tp: 8 (over y, core).
Axes of the slice: x: 4, y: 4, z: 4, core: 2. Of those that a mesh axis runs over, the one named last changes fastest.
Arguments:
- normed_hidden_input: bfloat16 [3, 2048, 8192], P(None, 'rep', 'tp'), may hold values from -6 to 6
- query_key_value_weight: bfloat16 [8192, 8, 1280], P(None, 'tp'), may hold values from -0.0625 to 0.0625
- adapter_down_weight: bfloat16 [128, 8192, 64], P('rep', 'tp'), may hold values from -0.0625 to 0.0625
- adapter_up_weight: bfloat16 [128, 64, 8, 1280], P('rep', None, 'tp'), may hold values from -0.75 to 0.75
- cached_rotated_keys: bfloat16 [2048, 8, 128, 128], P('rep', 'tp'), may hold values from -1000 to 1000
- cached_value_rows: bfloat16 [2048, 8, 128, 128], P('rep', 'tp'), may hold values from -6 to 6
- cached_length_valid: int32 [2048], P('rep'), may hold values from 2 to 128, as said below
- request_adapter: int32 [2048], P('rep'), may hold values from 0 to 127, as said below
- adapter_storage_slot: int32 [128], replicated, may hold values from 0 to 127, as said below
Outputs:
- attended: bfloat16 [3, 2048, 8192], P(None, 'rep', 'tp')
Inputs may be any that keep to these rules, and one draw needn't show every extreme that they name: `adapter_storage_slot`: each slot is used once; slots s * 8 to (s + 1) * 8 - 1 are stored on replica s. `request_adapter`: among the 128 requests of one replica, at most 32 use adapters stored on any one replica; in every draw some replica stores the adapters of exactly 32 requests of every replica. `cached_length_valid`: every replica has a request with 128 cached positions.
All inputs are finite; a program needn't handle non-finite values.
Results may differ from a plain program's by a relative error of at most 0.015.
Values may be sent and summed in bfloat16 or wider, within the bound.
A program may use at most 192 MiB of HBM per device.

v0:
```python
import jax
import jax.numpy as jnp
from jax import lax
from jax.sharding import PartitionSpec as P


def rotate(vector, position):
    half = vector.shape[-1] // 2
    freqs = jnp.exp(
        jnp.arange(half, dtype=jnp.float32)
        * (-2.0 / vector.shape[-1])
        * jnp.log(jnp.float32(500000.0))
    )
    angle = position[:, None] * freqs[None, :]
    target = (position.shape[0],) + (1,) * (vector.ndim - 2) + (half,)
    cosine = jnp.cos(angle).reshape(target)
    sine = jnp.sin(angle).reshape(target)
    first = vector[..., :half]
    second = vector[..., half:]
    return jnp.concatenate(
        [first * cosine - second * sine, second * cosine + first * sine], axis=-1
    )


def attend(
    query, cached_rotated_keys, cached_value_rows, fresh_keys, fresh_values, cached_length_valid
):
    factor = query.shape[-1] ** (-0.5)
    cache_scores = (
        jnp.einsum(
            "rhgd,rhpd->rhgp", query, cached_rotated_keys, preferred_element_type=jnp.float32
        )
        * factor
    )
    valid = (
        jnp.arange(cached_rotated_keys.shape[2], dtype=jnp.int32)[None, :]
        < cached_length_valid[:, None]
    )
    cache_scores = jnp.where(valid[:, None, None, :], cache_scores, -jnp.inf)
    fresh_scores = (
        jnp.einsum("rhgd,rhjd->rhgj", query, fresh_keys, preferred_element_type=jnp.float32)
        * factor
    )
    highest = jnp.maximum(jnp.max(cache_scores, axis=-1), jnp.max(fresh_scores, axis=-1))[..., None]
    cache_exp = jnp.exp(cache_scores - highest)
    fresh_exp = jnp.exp(fresh_scores - highest)
    denominator = jnp.sum(cache_exp, axis=-1, keepdims=True) + jnp.sum(
        fresh_exp, axis=-1, keepdims=True
    )
    cache_weights = (cache_exp / denominator).astype(jnp.bfloat16)
    fresh_weights = (fresh_exp / denominator).astype(jnp.bfloat16)
    mixed = jnp.einsum(
        "rhgp,rhpd->rhgd", cache_weights, cached_value_rows, preferred_element_type=jnp.float32
    )
    mixed = mixed + jnp.einsum(
        "rhgj,rhjd->rhgd", fresh_weights, fresh_values, preferred_element_type=jnp.float32
    )
    return mixed.astype(jnp.bfloat16)


def local(
    normed_hidden_input,
    query_key_value_weight,
    adapter_down_weight,
    adapter_up_weight,
    cached_rotated_keys,
    cached_value_rows,
    cached_length_valid,
    request_adapter,
    adapter_storage_slot,
):
    replicas = lax.axis_size("rep")
    step_count, row_count, width_part = normed_hidden_input.shape
    kv_local = query_key_value_weight.shape[1]
    joined_width = query_key_value_weight.shape[2]
    head_size = cached_rotated_keys.shape[3]
    group_size = joined_width // head_size - 2
    output_width = kv_local * joined_width
    owned_portion = adapter_down_weight.shape[0]
    rank_column_width = adapter_down_weight.shape[2]
    capacity = 4 * row_count // replicas
    adapter_count = adapter_storage_slot.shape[0]
    matches = request_adapter[:, None] == jnp.arange(adapter_count, dtype=jnp.int32)[None, :]
    slot_row = jnp.sum(jnp.where(matches, adapter_storage_slot[None, :], 0), axis=1)
    owner_row = slot_row // owned_portion
    within_row = slot_row % owned_portion
    owner_table = (owner_row[:, None] == jnp.arange(replicas, dtype=jnp.int32)[None, :]).astype(
        jnp.int32
    )
    order_within = jnp.sum((jnp.cumsum(owner_table, axis=0) - 1) * owner_table, axis=1)
    target_slot = owner_row * capacity + order_within
    placing = target_slot[None, :] == jnp.arange(replicas * capacity, dtype=jnp.int32)[:, None]
    place_matrix = placing.astype(jnp.bfloat16)
    slot_index = jnp.sum(jnp.where(placing, within_row[None, :] + 1, 0), axis=1) - 1
    weight = query_key_value_weight.reshape(query_key_value_weight.shape[0], output_width)
    up_weight_matrix = adapter_up_weight.reshape(owned_portion * rank_column_width, output_width)
    joined_list = []
    for step in range(step_count):
        base_step = jnp.dot(
            lax.all_gather(normed_hidden_input[step], "tp", axis=1, tiled=True),
            weight,
            preferred_element_type=jnp.float32,
        )
        block_rows = normed_hidden_input[step : step + 1]
        block_steps = block_rows.shape[0]
        outgoing = jnp.einsum(
            "sr,nrd->nsd", place_matrix, block_rows, preferred_element_type=jnp.float32
        )
        outgoing = outgoing.astype(jnp.bfloat16).reshape(
            block_steps, replicas, capacity, width_part
        )
        index_out = slot_index.reshape(1, replicas, capacity)
        arrived_rows = lax.all_to_all(outgoing, "rep", split_axis=1, concat_axis=1, tiled=True)
        arrived_index = lax.all_to_all(index_out, "rep", split_axis=1, concat_axis=1, tiled=True)
        item_count = arrived_rows.shape[0]
        flattened_rows = arrived_rows.reshape(item_count * replicas * capacity, width_part)
        picks = (
            arrived_index.reshape(-1)[:, None]
            == jnp.arange(owned_portion, dtype=jnp.int32)[None, :]
        ).astype(jnp.float32)
        projected = jnp.einsum(
            "nb,tbo->nto", flattened_rows, adapter_down_weight, preferred_element_type=jnp.float32
        )
        low_part = jnp.sum(projected * picks[:, :, None], axis=1)
        low_rounded = lax.psum(low_part, "tp").astype(jnp.bfloat16)
        spread = (picks.astype(jnp.bfloat16)[:, :, None] * low_rounded[:, None, :]).reshape(
            -1, owned_portion * rank_column_width
        )
        delta_rows = jnp.dot(spread, up_weight_matrix, preferred_element_type=jnp.float32).astype(
            jnp.bfloat16
        )
        delta_rows = delta_rows.reshape(item_count, replicas, capacity, output_width)
        returned = lax.all_to_all(delta_rows, "rep", split_axis=1, concat_axis=1, tiled=True)
        returned = returned.reshape(block_steps, replicas * capacity, output_width)
        joined_list.append(
            base_step
            + jnp.einsum("sr,nsc->nrc", place_matrix, returned, preferred_element_type=jnp.float32)[
                0
            ]
        )
    query_width = group_size * head_size
    fresh_key_list = []
    fresh_value_list = []
    results = []
    for step in range(step_count):
        joined = joined_list[step].reshape(row_count, kv_local, joined_width)
        position = cached_length_valid.astype(jnp.float32) + step
        query = rotate(
            joined[..., :query_width].reshape(row_count, kv_local, group_size, head_size), position
        ).astype(jnp.bfloat16)
        fresh_key_list.append(
            rotate(joined[..., query_width : query_width + head_size], position).astype(
                jnp.bfloat16
            )
        )
        fresh_value_list.append(joined[..., query_width + head_size :].astype(jnp.bfloat16))
        mixed = attend(
            query,
            cached_rotated_keys,
            cached_value_rows,
            jnp.stack(fresh_key_list, 2),
            jnp.stack(fresh_value_list, 2),
            cached_length_valid,
        )
        results.append(mixed.reshape(row_count, kv_local * group_size * head_size))
    return jnp.stack(results)


def solution(mesh):
    placed = (
        P(None, "rep", "tp"),
        P(None, "tp", None),
        P("rep", "tp", None),
        P("rep", None, "tp", None),
        P("rep", "tp", None, None),
        P("rep", "tp", None, None),
        P("rep"),
        P("rep"),
        P(),
    )
    return jax.shard_map(
        local, mesh=mesh, in_specs=placed, out_specs=P(None, "rep", "tp"), check_vma=False
    )
```

profile of v0, /device:TPU:0, one launch (start us, length us, event | category | flops | bytes accessed | tf_op | source)
XLA Modules:
  0.0 257.6 jit_solution(12557983773636660297)
XLA Ops:
  6.5 2.2 fusion.148
  10.9 8.0 %all-to-all-start = ((s32[1,16,32]{2,0,1:T(1,128)}), s32[1,16,32]{2,0,1:T(1,128)S(1)}, u32[]{:S(2)}, u32[]{:S(2)}) async-start(s32[1,16,32]{2,0,1:T(1,128)} %sub.86), calls=%async_computation | async-start | bytes 16384 | tf_op jit(solution)/shard_map/all_to_all | solution.py:114
  20.3 6.1 %all-to-all-done = s32[1,16,32]{2,0,1:T(1,128)S(1)} async-done(((s32[1,16,32]{2,0,1:T(1,128)}), s32[1,16,32]{2,0,1:T(1,128)S(1)}, u32[]{:S(2)}, u32[]{:S(2)}) %all-to-all-start) | async-done | bytes 2080 | tf_op jit(solution)/shard_map/all_to_all | solution.py:114
  26.4 3.7 %all-to-all-start.1 = ((bf16[1,16,32,1024]{3,2,0,1:T(8,128)(2,1)}), bf16[1,16,32,1024]{3,2,0,1:T(8,128)(2,1)S(1)}, u32[]{:S(2)}, u32[]{:S(2)}) async-start(bf16[1,16,32,1024]{3,2,0,1:T(8,128)(2,1)} %bitcast.7), calls=%async_computation.1 | async-start | bytes 2097152 | tf_op jit(solution)/shard_map/all_to_all | solution.py:113
  31.5 14.5 %all-to-all-done.1 = bf16[1,16,32,1024]{3,2,0,1:T(8,128)(2,1)S(1)} async-done(((bf16[1,16,32,1024]{3,2,0,1:T(8,128)(2,1)}), bf16[1,16,32,1024]{3,2,0,1:T(8,128)(2,1)S(1)}, u32[]{:S(2)}, u32[]{:S(2)}) %all-to-all-start.1) | async-done | bytes 1048608 | tf_op jit(solution)/shard_map/all_to_all | solution.py:113
  46.0 4.3 %all-to-all-start.3 = ((bf16[1,16,32,1024]{3,2,0,1:T(8,128)(2,1)}), bf16[1,16,32,1024]{3,2,0,1:T(8,128)(2,1)}, u32[]{:S(2)}, u32[]{:S(2)}) async-start(bf16[1,16,32,1024]{3,2,0,1:T(8,128)(2,1)} %bitcast.36), calls=%async_computation.3 | async-start | bytes 2097152 | tf_op jit(solution)/shard_map/all_to_all | solution.py:113
  50.3 1.4 convolution_convert_fusion.3
  51.8 13.7 %all-to-all-done.3 = bf16[1,16,32,1024]{3,2,0,1:T(8,128)(2,1)} async-done(((bf16[1,16,32,1024]{3,2,0,1:T(8,128)(2,1)}), bf16[1,16,32,1024]{3,2,0,1:T(8,128)(2,1)}, u32[]{:S(2)}, u32[]{:S(2)}) %all-to-all-start.3) | async-done | bytes 1048608 | tf_op jit(solution)/shard_map/all_to_all | solution.py:113
  65.5 4.3 %all-to-all-start.5 = ((bf16[1,16,32,1024]{3,2,0,1:T(8,128)(2,1)}), bf16[1,16,32,1024]{3,2,0,1:T(8,128)(2,1)}, u32[]{:S(2)}, u32[]{:S(2)}) async-start(bf16[1,16,32,1024]{3,2,0,1:T(8,128)(2,1)} %bitcast.65), calls=%async_computation.5 | async-start | bytes 2097152 | tf_op jit(solution)/shard_map/all_to_all | solution.py:113
  72.4 2.0 fusion.154
  74.4 2.3 fusion.155
  76.7 8.2 %all-to-all-done.5 = bf16[1,16,32,1024]{3,2,0,1:T(8,128)(2,1)} async-done(((bf16[1,16,32,1024]{3,2,0,1:T(8,128)(2,1)}), bf16[1,16,32,1024]{3,2,0,1:T(8,128)(2,1)}, u32[]{:S(2)}, u32[]{:S(2)}) %all-to-all-start.5) | async-done | bytes 1048608 | tf_op jit(solution)/shard_map/all_to_all | solution.py:113
  84.9 2.3 fusion.156
  88.3 29.5 %all-reduce.2 = (bf16[512,64]{0,1:T(8,128)(2,1)S(1)}, bf16[512,64]{0,1:T(8,128)(2,1)S(1)}, bf16[512,64]{0,1:T(8,128)(2,1)S(1)}) all-reduce(f32[512,64]{0,1:T(8,128)} %get-tuple-element.6, f32[512,64]{0,1:T(8,128)} %get-tuple-element.7, f32[512,64]{0,1:T(8,128)S(1)} %get-tuple-element.5), channel_id=1, replica_groups=mesh['rep'=16,'tp'=8] {'tp'}, use_global_device_ids=true, to_apply=%region_15.16 | all-reduce | flops 98304 | bytes 589824 | tf_op jit(solution)/shard_map/psum | solution.py:125
  117.9 1.6 broadcast_multiply_fusion.2
  119.5 1.9 convolution_convert_fusion.1
  121.4 5.6 %all-to-all-start.4 = ((bf16[1,16,32,1280]{3,2,0,1:T(8,128)(2,1)}), bf16[1,16,32,1280]{3,2,0,1:T(8,128)(2,1)S(1)}, u32[]{:S(2)}, u32[]{:S(2)}) async-start(bf16[1,16,32,1280]{3,2,0,1:T(8,128)(2,1)} %bitcast.259), calls=%async_computation.4 | async-start | bytes 2621440 | tf_op jit(solution)/shard_map/all_to_all | solution.py:133
  127.0 3.1 %convolution_convert_fusion.2 = bf16[512,1280]{1,0:T(8,128)(2,1)} fusion(bf16[512,512]{0,1:T(8,128)(2,1)} %bitcast.265, bf16[512,1280]{1,0:T(8,128)(2,1)S(1)} %bitcast.249), kind=kOutput, calls=%fused_computation.20 | convolution fusion | flops 671744000 | bytes 3145728 | tf_op jit(solution)/shard_map/dot_general | solution.py:129
  130.0 14.6 %all-to-all-done.4 = bf16[1,16,32,1280]{3,2,0,1:T(8,128)(2,1)S(1)} async-done(((bf16[1,16,32,1280]{3,2,0,1:T(8,128)(2,1)}), bf16[1,16,32,1280]{3,2,0,1:T(8,128)(2,1)S(1)}, u32[]{:S(2)}, u32[]{:S(2)}) %all-to-all-start.4) | async-done | bytes 1310752 | tf_op jit(solution)/shard_map/all_to_all | solution.py:133
  144.6 4.4 %all-to-all-start.2 = ((bf16[1,16,32,1280]{3,2,0,1:T(8,128)(2,1)}), bf16[1,16,32,1280]{3,2,0,1:T(8,128)(2,1)}, u32[]{:S(2)}, u32[]{:S(2)}) async-start(bf16[1,16,32,1280]{3,2,0,1:T(8,128)(2,1)} %bitcast.257), calls=%async_computation.2 | async-start | bytes 2621440 | tf_op jit(solution)/shard_map/all_to_all | solution.py:133
  149.9 2.0 convolution_convert_fusion
  151.8 14.9 %all-to-all-done.2 = bf16[1,16,32,1280]{3,2,0,1:T(8,128)(2,1)} async-done(((bf16[1,16,32,1280]{3,2,0,1:T(8,128)(2,1)}), bf16[1,16,32,1280]{3,2,0,1:T(8,128)(2,1)}, u32[]{:S(2)}, u32[]{:S(2)}) %all-to-all-start.2) | async-done | bytes 1310752 | tf_op jit(solution)/shard_map/all_to_all | solution.py:133
  166.7 3.9 %all-to-all-start.6 = ((bf16[1,16,32,1280]{3,2,0,1:T(8,128)(2,1)}), bf16[1,16,32,1280]{3,2,0,1:T(8,128)(2,1)S(1)}, u32[]{:S(2)}, u32[]{:S(2)}) async-start(bf16[1,16,32,1280]{3,2,0,1:T(8,128)(2,1)} %bitcast.258), calls=%async_computation.6 | async-start | bytes 2621440 | tf_op jit(solution)/shard_map/all_to_all | solution.py:133
  172.8 1.7 convolution_bitcast_fusion.2
  174.5 13.6 %all-to-all-done.6 = bf16[1,16,32,1280]{3,2,0,1:T(8,128)(2,1)S(1)} async-done(((bf16[1,16,32,1280]{3,2,0,1:T(8,128)(2,1)}), bf16[1,16,32,1280]{3,2,0,1:T(8,128)(2,1)S(1)}, u32[]{:S(2)}, u32[]{:S(2)}) %all-to-all-start.6) | async-done | bytes 1310752 | tf_op jit(solution)/shard_map/all_to_all | solution.py:133
  189.1 10.5 %fusion.30 = f32[128,1,1280]{2,0,1:T(8,128)S(1)} fusion(f32[128,1280]{1,0:T(8,128)S(1)} %convolution_bitcast_fusion.1, bf16[8192,1,1280]{2,0,1:T(8,128)(2,1)} %param.10, bf16[1,128,8192]{2,1,0:T(8,128)(2,1)} %all-gather.9.cloned.1.call-done), kind=kOutput, calls=%fused_computation.28 | convolution fusion | flops 2684518400 | bytes 24379392 | tf_op jit(solution)/shard_map/dot_general | solution.py:99
  199.7 10.5 %fusion.33 = f32[128,1,1280]{2,0,1:T(8,128)S(1)} fusion(f32[128,1280]{1,0:T(8,128)S(1)} %convolution_bitcast_fusion.2, bf16[8192,1,1280]{2,0,1:T(8,128)(2,1)} %param.10, bf16[1,128,8192]{2,1,0:T(8,128)(2,1)} %all-gather.7.cloned.1.call-done), kind=kOutput, calls=%fused_computation.29 | convolution fusion | flops 2684518400 | bytes 24379392 | tf_op jit(solution)/shard_map/dot_general | solution.py:99
  211.0 10.5 %fusion.27 = f32[128,1,1280]{2,0,1:T(8,128)S(1)} fusion(f32[128,1280]{1,0:T(8,128)S(1)} %convolution_bitcast_fusion, bf16[8192,1,1280]{2,0,1:T(8,128)(2,1)} %param.10, bf16[1,128,8192]{2,1,0:T(8,128)(2,1)} %all-gather.11.cloned.1.call-done), kind=kOutput, calls=%fused_computation.27 | convolution fusion | flops 2684518400 | bytes 24379392 | tf_op jit(solution)/shard_map/dot_general | solution.py:99
  225.0 4.6 %fusion.153 = (f32[128,8]{1,0:T(8,128)S(1)}, f32[128,8,128]{2,1,0:T(8,128)S(1)}) fusion(bf16[128,1,128,128]{3,2,1,0:T(8,128)(2,1)} %param.13, bf16[128,8,64]{2,1,0:T(8,128)(2,1)S(1)} %get-tuple-element.23, bf16[128,8,64]{2,1,0:T(8,128)(2,1)S(1)} %get-tuple-element.22, pred[128,128]{1,0:T(8,128)(4,1)S(1)} %iota_compare_fusion.9), kind=kOutput, calls=%fused_computation.209 | convolution fusion | flops 34470912 | bytes 5001216 | tf_op jit(solution)/shard_map/rhgd,rhpd->rhgp/dot_general | solution.py:30
  230.5 3.4 %fusion.62 = bf16[128,8,128]{2,1,0:T(8,128)(2,1)S(1)} fusion(bf16[128,1,128,128]{3,2,1,0:T(8,128)(2,1)} %param.14, f32[128,8,128]{2,1,0:T(8,128)S(1)} %get-tuple-element.62, f32[128,128]{1,0:T(8,128)S(1)} %copy-done.10, f32[128,8]{1,0:T(8,128)S(1)} %copy.74, f32[128,8]{1,0:T(8,128)S(1)} %copy.73, f32[128,8]{1,0:T(8,128)S(1)} %copy.71), kind=kOutput, calls=%fused_computation.47 | convolution fusion | flops 34340864 | bytes 5058560 | tf_op jit(solution)/shard_map/rhgp,rhpd->rhgd/dot_general | solution.py:52
  234.0 4.7 %fusion.151 = (f32[128,8]{1,0:T(8,128)S(1)}, f32[128,8,128]{2,1,0:T(8,128)S(1)}) fusion(bf16[128,1,128,128]{3,2,1,0:T(8,128)(2,1)} %param.13, bf16[128,8,64]{2,1,0:T(8,128)(2,1)S(1)} %get-tuple-element.63, bf16[128,8,64]{2,1,0:T(8,128)(2,1)S(1)} %get-tuple-element.64, pred[128,128]{1,0:T(8,128)(4,1)S(1)} %iota_compare_fusion.9), kind=kOutput, calls=%fused_computation.207 | convolution fusion | flops 34470912 | bytes 5001216 | tf_op jit(solution)/shard_map/rhgd,rhpd->rhgp/dot_general | solution.py:30
  242.5 4.7 %fusion.149 = (f32[128,8]{1,0:T(8,128)S(1)}, f32[128,8,128]{2,1,0:T(8,128)S(1)}) fusion(bf16[128,1,128,128]{3,2,1,0:T(8,128)(2,1)} %param.13, bf16[128,8,64]{2,1,0:T(8,128)(2,1)S(1)} %get-tuple-element.27, bf16[128,8,64]{2,1,0:T(8,128)(2,1)S(1)} %get-tuple-element.26, pred[128,128]{1,0:T(8,128)(4,1)S(1)} %iota_compare_fusion.9), kind=kOutput, calls=%fused_computation.205 | convolution fusion | flops 34470912 | bytes 5001216 | tf_op jit(solution)/shard_map/rhgd,rhpd->rhgp/dot_general | solution.py:30
  (121 shorter events, 25.1 us)
Async XLA Ops:
  6.5 112.9 %copy-start = (bf16[8,64,1,1280]{3,1,2,0:T(8,128)(2,1)S(1)}, bf16[8,64,1,1280]{3,1,2,0:T(8,128)(2,1)}, u32[]{:S(2)}) copy-start(bf16[8,64,1,1280]{3,1,2,0:T(8,128)(2,1)} %param.12) | copy-start | bytes 3932164
  6.5 12.4 %copy-start.4 = (bf16[3,128,1024]{2,1,0:T(8,128)(2,1)S(1)}, bf16[3,128,1024]{2,1,0:T(8,128)(2,1)}, u32[]{:S(2)}) copy-start(bf16[3,128,1024]{2,1,0:T(8,128)(2,1)} %param.9) | copy-start | bytes 2359300
  6.5 182.6 %all-gather.9.cloned.1.call-start = ((), (), s32[]{:S(2)}) async-start(), calls=%async_computation.8 | async-start | bytes 2359296 | tf_op jit(solution)/shard_map/all_gather | solution.py:100
  10.1 40.2 %copy-start.11 = (s32[128]{0:T(128)}, s32[128]{0:T(128)S(1)}, u32[]{:S(2)}) copy-start(s32[128]{0:T(128)S(1)} %multiply_add_fusion) | copy-start | bytes 1540
  10.9 15.5 %all-to-all-start = ((s32[1,16,32]{2,0,1:T(1,128)}), s32[1,16,32]{2,0,1:T(1,128)S(1)}, u32[]{:S(2)}, u32[]{:S(2)}) async-start(s32[1,16,32]{2,0,1:T(1,128)} %sub.86), calls=%async_computation | async-start | bytes 16384 | tf_op jit(solution)/shard_map/all_to_all | solution.py:114
  26.4 19.6 %all-to-all-start.1 = ((bf16[1,16,32,1024]{3,2,0,1:T(8,128)(2,1)}), bf16[1,16,32,1024]{3,2,0,1:T(8,128)(2,1)S(1)}, u32[]{:S(2)}, u32[]{:S(2)}) async-start(bf16[1,16,32,1024]{3,2,0,1:T(8,128)(2,1)} %bitcast.7), calls=%async_computation.1 | async-start | bytes 2097152 | tf_op jit(solution)/shard_map/all_to_all | solution.py:113
  46.0 19.5 %all-to-all-start.3 = ((bf16[1,16,32,1024]{3,2,0,1:T(8,128)(2,1)}), bf16[1,16,32,1024]{3,2,0,1:T(8,128)(2,1)}, u32[]{:S(2)}, u32[]{:S(2)}) async-start(bf16[1,16,32,1024]{3,2,0,1:T(8,128)(2,1)} %bitcast.36), calls=%async_computation.3 | async-start | bytes 2097152 | tf_op jit(solution)/shard_map/all_to_all | solution.py:113
  65.5 19.5 %all-to-all-start.5 = ((bf16[1,16,32,1024]{3,2,0,1:T(8,128)(2,1)}), bf16[1,16,32,1024]{3,2,0,1:T(8,128)(2,1)}, u32[]{:S(2)}, u32[]{:S(2)}) async-start(bf16[1,16,32,1024]{3,2,0,1:T(8,128)(2,1)} %bitcast.65), calls=%async_computation.5 | async-start | bytes 2097152 | tf_op jit(solution)/shard_map/all_to_all | solution.py:113
  69.8 129.8 %all-gather.7.cloned.1.call-start = ((), (), s32[]{:S(2)}) async-start(), calls=%async_computation.7 | async-start | bytes 2359296 | tf_op jit(solution)/shard_map/all_gather | solution.py:100
  121.4 23.3 %all-to-all-start.4 = ((bf16[1,16,32,1280]{3,2,0,1:T(8,128)(2,1)}), bf16[1,16,32,1280]{3,2,0,1:T(8,128)(2,1)S(1)}, u32[]{:S(2)}, u32[]{:S(2)}) async-start(bf16[1,16,32,1280]{3,2,0,1:T(8,128)(2,1)} %bitcast.259), calls=%async_computation.4 | async-start | bytes 2621440 | tf_op jit(solution)/shard_map/all_to_all | solution.py:133
  130.0 19.8 %copy-start.21 = (s32[128]{0:T(128)S(1)}, s32[128]{0:T(128)}, u32[]{:S(2)}) copy-start(s32[128]{0:T(128)} %param.15) | copy-start | bytes 1540
  144.6 22.1 %all-to-all-start.2 = ((bf16[1,16,32,1280]{3,2,0,1:T(8,128)(2,1)}), bf16[1,16,32,1280]{3,2,0,1:T(8,128)(2,1)}, u32[]{:S(2)}, u32[]{:S(2)}) async-start(bf16[1,16,32,1280]{3,2,0,1:T(8,128)(2,1)} %bitcast.257), calls=%async_computation.2 | async-start | bytes 2621440 | tf_op jit(solution)/shard_map/all_to_all | solution.py:133
  149.1 61.9 %all-gather.11.cloned.1.call-start = ((), (), s32[]{:S(2)}) async-start(), calls=%async_computation.9 | async-start | bytes 2359296 | tf_op jit(solution)/shard_map/all_gather | solution.py:100
  149.8 20.9 %copy-start.13 = (f32[128]{0:T(128)}, f32[128]{0:T(128)S(1)}, u32[]{:S(2)}) copy-start(f32[128]{0:T(128)S(1)} %convert_element_type.178) | copy-start | bytes 1540
  149.8 20.9 %copy-start.15 = (f32[64]{0:T(128)}, f32[64]{0:T(128)S(1)}, u32[]{:S(2)}) copy-start(f32[64]{0:T(128)S(1)} %multiply_exponential_fusion) | copy-start | bytes 772
  166.7 21.4 %all-to-all-start.6 = ((bf16[1,16,32,1280]{3,2,0,1:T(8,128)(2,1)}), bf16[1,16,32,1280]{3,2,0,1:T(8,128)(2,1)S(1)}, u32[]{:S(2)}, u32[]{:S(2)}) async-start(bf16[1,16,32,1280]{3,2,0,1:T(8,128)(2,1)} %bitcast.258), calls=%async_computation.6 | async-start | bytes 2621440 | tf_op jit(solution)/shard_map/all_to_all | solution.py:133
  170.6 2.1 copy-start.12
  170.6 1.1 copy-start.17
  170.7 1.1 copy-start.19
  210.9 10.5 %copy-start.14 = (f32[128]{0:T(128)S(1)}, f32[128]{0:T(128)}, u32[]{:S(2)}) copy-start(f32[128]{0:T(128)} %copy-done.13) | copy-start | bytes 1540
  210.9 10.5 %copy-start.16 = (f32[64]{0:T(128)S(1)}, f32[64]{0:T(128)}, u32[]{:S(2)}) copy-start(f32[64]{0:T(128)} %copy-done.15) | copy-start | bytes 772
  210.9 10.5 %copy-start.18 = (f32[128]{0:T(128)S(1)}, f32[128]{0:T(128)}, u32[]{:S(2)}) copy-start(f32[128]{0:T(128)} %copy-done.17) | copy-start | bytes 1540
  211.0 10.5 %copy-start.20 = (f32[128]{0:T(128)S(1)}, f32[128]{0:T(128)}, u32[]{:S(2)}) copy-start(f32[128]{0:T(128)} %copy-done.19) | copy-start | bytes 1540
  221.5 2.4 copy-start.5
  221.5 2.4 copy-start.6
  224.9 5.5 %copy-start.10 = (f32[128,128]{1,0:T(8,128)S(1)}, f32[128,128]{1,0:T(8,128)}, u32[]{:S(2)}) copy-start(f32[128,128]{1,0:T(8,128)} %get-tuple-element.20) | copy-start | bytes 196612
  234.0 5.9 %copy-start.2 = (bf16[128,1,128,128]{3,2,1,0:T(8,128)(2,1)S(1)}, bf16[128,1,128,128]{3,2,1,0:T(8,128)(2,1)}, u32[]{:S(2)}) copy-start(bf16[128,1,128,128]{3,2,1,0:T(8,128)(2,1)} %param.14) | copy-start | bytes 12582916
  241.2 0.8 copy-start.9
  241.2 0.9 copy-start.7
  241.3 0.9 copy-start.8
  242.5 5.8 %copy-start.3 = (bf16[128,1,128,128]{3,2,1,0:T(8,128)(2,1)S(1)}, bf16[128,1,128,128]{3,2,1,0:T(8,128)(2,1)}, u32[]{:S(2)}) copy-start(bf16[128,1,128,128]{3,2,1,0:T(8,128)(2,1)} %param.14) | copy-start | bytes 12582916
  248.3 2.7 %copy-start.1 = (bf16[8,64,1,1280]{3,1,2,0:T(8,128)(2,1)S(1)}, bf16[8,64,1,1280]{3,1,2,0:T(8,128)(2,1)}, u32[]{:S(2)}) copy-start(bf16[8,64,1,1280]{3,1,2,0:T(8,128)(2,1)} %param.12) | copy-start | bytes 3932164
Sparse Core Ops, SparseCore 0:
  9.1 27.6 all-gather.8
  72.4 27.3 all-gather.6
  151.6 27.7 all-gather.10
where the time goes:
time: 263 us; the launch traced here: 258 us
  waiting for transfers between devices  87 us (33%)
  matrix products  74.9 us (28%)
  starting transfers between devices  34.2 us (13%)
  blocking collectives  29.5 us (11%)
  between operations  13.8 us (5%)
  other arithmetic  12.4 us (5%)
  local copies, waits for them, and re-layouts  5.69 us (2%)
    all_to_all x3, waiting for transfers between devices, local(): lax.all_to_all(delta_rows, 'rep', split_axis=1, concat_axis=1, tiled=True)  43.1 us
    all_to_all x3, waiting for transfers between devices, local(): lax.all_to_all(outgoing, 'rep', split_axis=1, concat_axis=1, tiled=True)  36.4 us
    dot_general x3, matrix products, local(): jnp.dot(lax.all_gather(normed_hidden_input[step], 'tp', axis=1, tiled=Tru...  31.4 us
    psum x1, blocking collectives, local(): low_rounded = lax.psum(low_part, 'tp').astype(jnp.bfloat16)  29.5 us
    dot_general x3, matrix products, attend(): jnp.einsum('rhgd,rhpd->rhgp', query, cached_rotated_keys, preferred_eleme...  14.1 us
    all_to_all x3, starting transfers between devices, local(): lax.all_to_all(delta_rows, 'rep', split_axis=1, concat_axis=1, tiled=True)  13.9 us
    all_to_all x3, starting transfers between devices, local(): lax.all_to_all(outgoing, 'rep', split_axis=1, concat_axis=1, tiled=True)  12.3 us
    all_to_all x1, starting transfers between devices, local(): lax.all_to_all(index_out, 'rep', split_axis=1, concat_axis=1, tiled=True)  7.96 us
  transfers between devices with their start and end apart: 10, of which 7 were waited for; matrix products, arithmetic and copies ran while one was open for 20% of the time, Pallas kernels for 0%

commit v1 on v0

v1 whole, which is shorter than its diff:
```python
import functools

import jax
import jax.numpy as jnp
import numpy as np
from jax import lax
from jax.experimental import pallas as pl
from jax.experimental.pallas import tpu as pltpu
from jax.sharding import PartitionSpec as P

MESH = pl.DeviceIdType.MESH
F32 = jnp.float32
BF16 = jnp.bfloat16
STEPS = 3
REQS = 128
ROWS = STEPS * REQS
WIDTH = 1024
OUT = 1280
RANKS = 512
CHUNK = 256
CHUNKS = OUT // CHUNK
HALF = ROWS // 2
PACK = ROWS // 2
PART = PACK // 8
PARTPAD = 32
QROWS = 24


def dot(a, b):
    return jnp.dot(a, b, preferred_element_type=F32)


def dot_nt(a, b):
    return lax.dot_general(a, b, (((1,), (1,)), ((), ())), preferred_element_type=F32)


def column(row):
    return jnp.transpose(jnp.broadcast_to(row, (128, 128)))


def project(
    hid,
    weight,
    down,
    up,
    req_ref,
    table_ref,
    len_ref,
    query_out,
    key_out,
    value_out,
    xs,
    rows,
    downs,
    ups,
    wbuf,
    base,
    spread,
    acc,
    reqs,
    slots,
    cosine,
    sine,
    home,
    home_in,
    part_in,
    low_part,
    low_parts,
    low_own,
    lows,
    dsend,
    relay_in,
    back_in,
    ssem,
    rsem,
    lsem,
):
    rep = lax.axis_index("rep")
    tp = lax.axis_index("tp")
    x, z, y, c = rep // 4, rep % 4, tp // 2, tp % 2
    r = z * (1 - c) + x * c
    w = x * (1 - c) + z * c

    def rep_at(r_, w_):
        return (w_ * (1 - c) + r_ * c) * 4 + r_ * (1 - c) + w_ * c

    def dev(rep_, tp_):
        return {"rep": rep_, "tp": tp_}

    shift = (0, 3, 1, 2)
    row_reps = [rep_at((r + s) % 4, w) for s in shift]
    weight_reps = [rep_at(r, (w + s) % 4) for s in shift]
    row_dev = [dev(q, tp) for q in row_reps]
    weight_dev = [dev(q, tp) for q in weight_reps]
    tps = [((y + s) % 4) * 2 + c for s in shift]
    sib_tps = [((y + s) % 4) * 2 + 1 - c for s in shift]
    y_dev = [dev(rep, q) for q in tps]
    sibling = dev(rep, sib_tps[0])
    tp_dev = [dev(rep, (tp + k) % 8) for k in range(8)]

    count = [0]

    def remote(src, dst, device):
        i = count[0]
        count[0] += 1
        return pltpu.make_async_remote_copy(
            src_ref=src,
            dst_ref=dst,
            send_sem=ssem.at[i],
            recv_sem=rsem.at[i],
            device_id=device,
            device_id_type=MESH,
        )

    lcount = [0]

    def local(src, dst):
        i = lcount[0]
        lcount[0] += 1
        return pltpu.make_async_copy(src, dst, lsem.at[i])

    sent = []

    def go(*copies):
        for cp in copies:
            cp.start()
            sent.append(cp)

    class Ring:
        def __init__(self, src, slot, size, devs):
            a, b = pl.ds(0, size // 2), pl.ds(size // 2, size // 2)
            left, right = devs[1], devs[2]
            self.first = [
                remote(src(a), slot(1, a), right),
                remote(src(b), slot(2, b), left),
            ]
            self.second = [
                remote(src(b), slot(1, b), right),
                remote(src(a), slot(2, a), left),
            ]
            self.far = [
                remote(slot(1, a), slot(3, a), right),
                remote(slot(2, b), slot(3, b), left),
            ]

        def relay(self):
            for i in range(2):
                self.first[i].wait_recv()
                go(self.far[i])

        def near(self):
            for i in range(2):
                self.second[i].wait_recv()

        def rest(self):
            for i in range(2):
                self.far[i].wait_recv()

    load_rows = local(hid, rows.at[0])
    load_down = local(down, downs.at[0])
    load_up = local(up, ups.at[0])
    order = [(i, s) for i in range(4) for s in range(2)]
    load_w = []
    for i, s in order:
        t_ = (tps if s == 0 else sib_tps)[i]
        load_w.append(
            local(weight.at[pl.ds(pl.multiple_of(t_ * WIDTH, WIDTH), WIDTH), :], wbuf.at[i * 2 + s])
        )
    load_rows.start()
    load_down.start()
    load_w[0].start()
    load_w[1].start()

    reqs[0] = jnp.broadcast_to(req_ref[...], (8, 128))

    barrier = pltpu.get_barrier_semaphore()
    peers = [row_dev[1], row_dev[2], row_dev[3], weight_dev[1], weight_dev[2]] + tp_dev[1:]
    for peer in peers:
        pl.semaphore_signal(barrier, inc=1, device_id=peer, device_id_type=MESH)
    pl.semaphore_wait(barrier, len(peers))

    y_ring = Ring(lambda h: hid.at[h], lambda s, h: xs.at[2 * s, h], ROWS, y_dev)
    r_ring = Ring(lambda h: hid.at[h], lambda s, h: rows.at[s, h], ROWS, row_dev)
    w_ring = Ring(lambda h: down.at[h], lambda s, h: downs.at[s, h], RANKS, weight_dev)
    up_rings = []
    for k in range(CHUNKS):
        cols = pl.ds(k * CHUNK, CHUNK)
        up_rings.append(
            Ring(
                lambda h, cols=cols: up.at[h, cols],
                lambda s, h, cols=cols: ups.at[s, h, cols],
                RANKS,
                weight_dev,
            )
        )
    req_copies = [remote(reqs.at[0], reqs.at[(0, 2, 1, 3)[i]], row_dev[i]) for i in (1, 2, 3)]
    sib_copies = [remote(hid, xs.at[1], sibling)] + [
        remote(xs.at[2 * i], xs.at[2 * i + 1], sibling) for i in (1, 2, 3)
    ]

    go(*req_copies)
    go(*w_ring.first, *r_ring.first, *y_ring.first)
    go(*w_ring.second, *r_ring.second, *y_ring.second)
    go(sib_copies[0])
    for cp in load_w[2:]:
        cp.start()
    load_up.start()

    lane = lax.broadcasted_iota(jnp.int32, (128, 128), 1)
    low_lane = lane < 64

    freq = jnp.exp((lane % 64).astype(F32) * (-2.0 / 128) * jnp.log(F32(500000.0)))
    pos = column(len_ref[...]).astype(F32)
    for t in range(STEPS):
        angle = (pos + t) * freq
        part = pl.ds(t * REQS, REQS)
        cosine[part, :] = jnp.cos(angle)
        sine[part, :] = jnp.where(low_lane, -1.0, 1.0) * jnp.sin(angle)

    def rotate(v):
        return v * cosine[...] + pltpu.roll(v, 64, 1) * sine[...]

    def find_slots(i):
        hit = column(reqs[i, 0:1, :]) == lane
        found = jnp.sum(
            jnp.where(hit, jnp.broadcast_to(table_ref[...], (128, 128)), 0).astype(F32),
            axis=1,
            keepdims=True,
        )
        slots[i] = jnp.broadcast_to(found, (128, 128)).astype(jnp.int32)

    find_slots(0)

    def base_mm(x_ref, j, first=False):
        load_w[j].wait()

        @pl.loop(0, CHUNKS)
        def _(n):
            cols = pl.ds(pl.multiple_of(n * CHUNK, CHUNK), CHUNK)
            got = dot(x_ref[...], wbuf[j, :, cols])
            if first:
                base[:, cols] = got
            else:
                base[:, cols] += got

    def down_mm(i, j):
        @pl.loop(0, 2)
        def _(h):
            part = pl.ds(pl.multiple_of(h * 256, 256), 256)
            got = dot_nt(rows[i], downs[j, part, :])
            for p in range(2):
                target = weight_reps[j] * 8 + h * 4 + 2 * p + jnp.where(low_lane, 0, 1)
                hit = slots[i] == target
                for t in range(STEPS):
                    tt = pl.ds(t * REQS, REQS)
                    acc[i, tt, :] += jnp.where(
                        hit, got[t * REQS : (t + 1) * REQS, p * 128 : (p + 1) * 128], 0.0
                    )

    acc[...] = jnp.zeros_like(acc)
    load_rows.wait()
    base_mm(rows.at[0], 0, first=True)
    load_down.wait()
    down_mm(0, 0)
    for cp in req_copies:
        cp.wait_recv()
    for i in (1, 2, 3):
        find_slots(i)
    sib_copies[0].wait_recv()
    base_mm(xs.at[1], 1)

    y_ring.relay()
    r_ring.relay()
    w_ring.relay()

    y_ring.near()
    go(sib_copies[1], sib_copies[2])
    r_ring.near()
    down_mm(1, 0)
    down_mm(2, 0)
    base_mm(xs.at[2], 2)
    w_ring.near()
    go(*up_rings[0].first, *up_rings[0].second)
    for j in (1, 2):
        for i in (0, 1, 2):
            down_mm(i, j)
    y_ring.rest()
    go(sib_copies[3])
    r_ring.rest()
    for j in (0, 1, 2):
        down_mm(3, j)
    w_ring.rest()
    go(*up_rings[1].first, *up_rings[1].second)
    go(*up_rings[2].first, *up_rings[2].second)
    for i in (3, 1, 2, 0):
        down_mm(i, 3)

    home_copies = []
    for i in range(4):
        both = acc[i] + pltpu.roll(acc[i], 64, 1)
        lane_h = lax.broadcasted_iota(jnp.int32, (PACK, 128), 1) < 64
        home[i] = jnp.where(lane_h, both[:PACK], both[PACK:])
        if i:
            cp = remote(home.at[i], home_in.at[(0, 2, 1, 3)[i]], row_dev[i])
            home_copies.append(cp)
            go(cp)
    up_rings[0].relay()
    for cp in home_copies:
        cp.wait_recv()
    home[0] = (home[0] + home_in[1]) + (home_in[2] + home_in[3])
    part_copies = []
    for k in range(1, 8):
        target = (tp + k) % 8
        cp = remote(
            home.at[0, pl.ds(pl.multiple_of(target * PART, 8), PART), :], part_in.at[k], tp_dev[k]
        )
        part_copies.append(cp)
        go(cp)
    go(*up_rings[3].first, *up_rings[3].second)
    up_rings[1].relay()
    for i in (1, 2):
        sib_copies[i].wait_recv()
    base_mm(xs.at[4], 4)
    for cp in part_copies:
        cp.wait_recv()
    total = home[0, pl.ds(pl.multiple_of(tp * PART, 8), PART), :]
    for k in range(1, 8):
        total = total + part_in[k]
    low_part[...] = jnp.concatenate([total, jnp.zeros((PARTPAD - PART, 128), F32)], 0).astype(BF16)
    low_copies = []
    for k in range(1, 8):
        cp = remote(low_part, low_parts.at[k], tp_dev[k])
        low_copies.append(cp)
        go(cp)
    go(*up_rings[4].first, *up_rings[4].second)
    up_rings[2].relay()
    base_mm(xs.at[3], 3)
    for cp in low_copies:
        cp.wait_recv()
    low_own[pl.ds(pl.multiple_of(tp * PART, 8), PART), :] = low_part[...].astype(F32)[:PART]
    for k in range(1, 8):
        source = (tp + 8 - k) % 8
        low_own[pl.ds(pl.multiple_of(source * PART, 8), PART), :] = low_parts[k].astype(F32)[:PART]
    lows[0] = low_own[...].astype(BF16)
    back_low = [remote(lows.at[0], lows.at[(0, 2, 1, 3)[i]], row_dev[i]) for i in (1, 2, 3)]
    go(*back_low)

    def spread_rows(i):
        packed = lows[i].astype(F32)
        turned = pltpu.roll(packed, 64, 1)
        lane_h = lax.broadcasted_iota(jnp.int32, (PACK, 128), 1) < 64
        low = jnp.concatenate(
            [jnp.where(lane_h, packed, turned), jnp.where(lane_h, turned, packed)], 0
        )
        for j in range(4):
            for p in range(4):
                target = weight_reps[j] * 8 + 2 * p + jnp.where(low_lane, 0, 1)
                hit = slots[i] == target
                for t in range(STEPS):
                    tt = slice(t * REQS, (t + 1) * REQS)
                    spread[i, tt, (j * 4 + p) * 128 : (j * 4 + p + 1) * 128] = jnp.where(
                        hit, low[tt], 0.0
                    ).astype(BF16)

    spread_rows(0)
    up_rings[3].relay()
    base_mm(xs.at[5], 5)
    for cp in back_low:
        cp.wait_recv()
    for i in (3, 1, 2):
        spread_rows(i)
    load_up.wait()

    order_c = (4, 0, 1, 2, 3)

    def delta(i, k):
        total = None
        for j in range(4):
            got = dot(spread[i, :, j * RANKS : (j + 1) * RANKS], ups[j, :, k * CHUNK : (k + 1) * CHUNK])
            total = got if total is None else total + got
        dsend[i, k] = total.astype(BF16)

    ha, hb = pl.ds(0, HALF), pl.ds(HALF, HALF)
    far_back, near_back, late_back = {}, {}, {}

    def send_chunk(k):
        up_rings[k].near()
        up_rings[k].rest()
        delta(3, k)
        far_back[k] = [
            remote(dsend.at[3, k, ha], relay_in.at[0, k], row_dev[2]),
            remote(dsend.at[3, k, hb], relay_in.at[1, k], row_dev[1]),
        ]
        go(*far_back[k])
        delta(1, k)
        delta(2, k)
        near_back[k] = [
            remote(dsend.at[2, k, hb], back_in.at[0, k, hb], row_dev[2]),
            remote(dsend.at[1, k, ha], back_in.at[1, k, ha], row_dev[1]),
        ]
        go(*near_back[k])
        delta(0, k)

    def relay_chunk(k):
        far_back[k][0].wait_recv()
        dsend[2, k, ha, :] = dsend[2, k, ha, :] + relay_in[0, k]
        far_back[k][1].wait_recv()
        dsend[1, k, hb, :] = dsend[1, k, hb, :] + relay_in[1, k]
        late_back[k] = [
            remote(dsend.at[2, k, ha], back_in.at[0, k, ha], row_dev[2]),
            remote(dsend.at[1, k, hb], back_in.at[1, k, hb], row_dev[1]),
        ]
        go(*late_back[k])

    def finish_chunk(k):
        for cp in near_back[k] + late_back[k]:
            cp.wait_recv()
        add = (dsend[0, k].astype(F32) + back_in[0, k].astype(F32)) + back_in[1, k].astype(F32)
        joined = base[:, k * CHUNK : (k + 1) * CHUNK] + add
        if k == CHUNKS - 1:
            key = rotate(joined[:, :128])
            for t in range(STEPS):
                tt = slice(t * REQS, (t + 1) * REQS)
                key_out[pl.ds(t, REQS, stride=8), :] = key[tt]
                value_out[pl.ds(t, REQS, stride=8), :] = joined[tt, 128:]
        else:
            for g in range(2):
                query = rotate(joined[:, g * 128 : (g + 1) * 128])
                for t in range(STEPS):
                    tt = slice(t * REQS, (t + 1) * REQS)
                    query_out[pl.ds(t * 8 + 2 * k + g, REQS, stride=QROWS), :] = query[tt]

    key_out[...] = jnp.zeros_like(key_out)
    value_out[...] = jnp.zeros_like(value_out)
    o = (0, 1, 2, 3, 4)
    up_rings[4].relay()
    send_chunk(o[0])
    send_chunk(o[1])
    sib_copies[3].wait_recv()
    base_mm(xs.at[6], 6)
    base_mm(xs.at[7], 7)
    relay_chunk(o[0])
    send_chunk(o[2])
    relay_chunk(o[1])
    finish_chunk(o[0])
    send_chunk(o[3])
    relay_chunk(o[2])
    finish_chunk(o[1])
    send_chunk(o[4])
    relay_chunk(o[3])
    finish_chunk(o[2])
    relay_chunk(o[4])
    finish_chunk(o[3])
    finish_chunk(o[4])
    for cp in sent:
        cp.wait_send()


BLOCK = 16


def attend(lens, query, key, value, keys, values, out, mixed, scores):
    step = pl.program_id(0)
    rows = BLOCK * QROWS
    factor = 128**-0.5
    q = query[...].astype(BF16)
    row = lax.broadcasted_iota(jnp.int32, (rows, 128), 0)
    lane = lax.broadcasted_iota(jnp.int32, (rows, 128), 1)
    fresh = dot_nt(q, key[...].astype(BF16)) * factor
    open_ = (row // QROWS == lane // 8) & (lane % 8 <= (row % QROWS) // 8)
    fresh = jnp.where(open_, fresh, -jnp.inf)
    lane_q = lax.broadcasted_iota(jnp.int32, (QROWS, 128), 1)
    for i in range(BLOCK):
        part = pl.ds(i * QROWS, QROWS)
        got = dot_nt(q[i * QROWS : (i + 1) * QROWS], keys[i]) * factor
        scores[part, :] = jnp.where(lane_q < lens[step * BLOCK + i], got, -jnp.inf)
    cached = scores[...]
    highest = jnp.max(jnp.maximum(cached, fresh), axis=1, keepdims=True)
    cached = jnp.exp(cached - highest)
    fresh = jnp.exp(fresh - highest)
    total = jnp.sum(cached + fresh, axis=1, keepdims=True)
    cached = (cached / total).astype(BF16)
    fresh = (fresh / total).astype(BF16)
    mixed[...] = dot(fresh, value[...].astype(BF16))
    for i in range(BLOCK):
        part = pl.ds(i * QROWS, QROWS)
        mixed[part, :] += dot(cached[i * QROWS : (i + 1) * QROWS], values[i])
    for t in range(STEPS):
        for g in range(8):
            out[t, :, g * 128 : (g + 1) * 128] = mixed[
                pl.ds(t * 8 + g, BLOCK, stride=QROWS), :
            ].astype(BF16)


def local(
    normed_hidden_input,
    query_key_value_weight,
    adapter_down_weight,
    adapter_up_weight,
    cached_rotated_keys,
    cached_value_rows,
    cached_length_valid,
    request_adapter,
    adapter_storage_slot,
):
    hid = normed_hidden_input.reshape(ROWS, WIDTH)
    weight = query_key_value_weight.reshape(8 * WIDTH, OUT)
    down = jnp.swapaxes(adapter_down_weight, 1, 2).reshape(RANKS, WIDTH)
    up = adapter_up_weight.reshape(RANKS, OUT)
    anywhere = pl.BlockSpec(memory_space=pl.ANY)
    in_vmem = pl.BlockSpec(memory_space=pltpu.VMEM)
    copies = 140
    query, key, value = pl.pallas_call(
        project,
        out_shape=(
            jax.ShapeDtypeStruct((REQS * QROWS, 128), F32),
            jax.ShapeDtypeStruct((REQS * 8, 128), F32),
            jax.ShapeDtypeStruct((REQS * 8, 128), F32),
        ),
        in_specs=[anywhere] * 4 + [in_vmem] * 3,
        out_specs=(in_vmem, in_vmem, in_vmem),
        scratch_shapes=[
            pltpu.VMEM((8, ROWS, WIDTH), BF16),
            pltpu.VMEM((4, ROWS, WIDTH), BF16),
            pltpu.VMEM((4, RANKS, WIDTH), BF16),
            pltpu.VMEM((4, RANKS, OUT), BF16),
            pltpu.VMEM((8, WIDTH, OUT), BF16),
            pltpu.VMEM((ROWS, OUT), F32),
            pltpu.VMEM((4, ROWS, 4 * RANKS), BF16),
            pltpu.VMEM((4, ROWS, 128), F32),
            pltpu.VMEM((4, 8, 128), jnp.int32),
            pltpu.VMEM((4, 128, 128), jnp.int32),
            pltpu.VMEM((ROWS, 128), F32),
            pltpu.VMEM((ROWS, 128), F32),
            pltpu.VMEM((4, PACK, 128), F32),
            pltpu.VMEM((4, PACK, 128), F32),
            pltpu.VMEM((8, PART, 128), F32),
            pltpu.VMEM((PARTPAD, 128), BF16),
            pltpu.VMEM((8, PARTPAD, 128), BF16),
            pltpu.VMEM((PACK, 128), F32),
            pltpu.VMEM((4, PACK, 128), BF16),
            pltpu.VMEM((4, CHUNKS, ROWS, CHUNK), BF16),
            pltpu.VMEM((2, CHUNKS, HALF, CHUNK), BF16),
            pltpu.VMEM((2, CHUNKS, ROWS, CHUNK), BF16),
            pltpu.SemaphoreType.DMA((copies,)),
            pltpu.SemaphoreType.DMA((copies,)),
            pltpu.SemaphoreType.DMA((16,)),
        ],
        compiler_params=pltpu.CompilerParams(
            collective_id=0, has_side_effects=True, vmem_limit_bytes=62 << 20
        ),
    )(
        hid,
        weight,
        down,
        up,
        request_adapter.reshape(1, REQS),
        adapter_storage_slot.reshape(1, 128),
        cached_length_valid.reshape(1, REQS),
    )
    keys = cached_rotated_keys.reshape(REQS, 128, 128)
    values = cached_value_rows.reshape(REQS, 128, 128)
    return pl.pallas_call(
        attend,
        out_shape=jax.ShapeDtypeStruct((STEPS, REQS, 1024), BF16),
        grid_spec=pltpu.PrefetchScalarGridSpec(
            num_scalar_prefetch=1,
            grid=(REQS // BLOCK,),
            in_specs=[
                pl.BlockSpec((BLOCK * QROWS, 128), lambda i, n: (i, 0)),
                pl.BlockSpec((BLOCK * 8, 128), lambda i, n: (i, 0)),
                pl.BlockSpec((BLOCK * 8, 128), lambda i, n: (i, 0)),
                pl.BlockSpec((BLOCK, 128, 128), lambda i, n: (i, 0, 0)),
                pl.BlockSpec((BLOCK, 128, 128), lambda i, n: (i, 0, 0)),
            ],
            out_specs=pl.BlockSpec((STEPS, BLOCK, 1024), lambda i, n: (0, i, 0)),
            scratch_shapes=[
                pltpu.VMEM((BLOCK * QROWS, 128), F32),
                pltpu.VMEM((BLOCK * QROWS, 128), F32),
            ],
        ),
    )(cached_length_valid, query, key, value, keys, values)


def solution(mesh):
    placed = (
        P(None, "rep", "tp"),
        P(None, "tp", None),
        P("rep", "tp", None),
        P("rep", None, "tp", None),
        P("rep", "tp", None, None),
        P("rep", "tp", None, None),
        P("rep"),
        P("rep"),
        P(),
    )
    return jax.shard_map(
        local, mesh=mesh, in_specs=placed, out_specs=P(None, "rep", "tp"), check_vma=False
    )
```

time: 263 us -> 108 us (0.41); the launches traced: 258 us -> 108 us
  Pallas kernels: 0 us -> 108 us
  waiting for transfers between devices: 87 us -> 0 us
  matrix products: 74.9 us -> 0 us
  starting transfers between devices: 34.2 us -> 0 us
  blocking collectives: 29.5 us -> 0 us
  between operations: 13.8 us -> 0.01 us
  other arithmetic: 12.4 us -> 0 us
  local copies, waits for them, and re-layouts: 5.69 us -> 0 us
    pallas_call x0 -> x2, Pallas kernels: none -> 108 us  [the longest x1 96.3 us: local(): pl.pallas_call(project, out_shape=(jax.ShapeDtypeStruct((REQS * QROWS, 12...]
    all_to_all x7 -> x0, waiting for transfers between devices: 85.6 us -> none  [the longest x3 43.1 us: local(): lax.all_to_all(delta_rows, 'rep', split_axis=1, concat_axis=1, tiled=True)]
    dot_general x23 -> x0, matrix products: 68.4 us -> none  [the longest x3 31.4 us: local(): jnp.dot(lax.all_gather(normed_hidden_input[step], 'tp', axis=1, tiled=Tru...]
    all_to_all x7 -> x0, starting transfers between devices: 34.2 us -> none  [the longest x3 13.9 us: local(): lax.all_to_all(delta_rows, 'rep', split_axis=1, concat_axis=1, tiled=True)]
    psum x1 -> x0, blocking collectives: 29.5 us -> none  [local(): low_rounded = lax.psum(low_part, 'tp').astype(jnp.bfloat16)]
    unnamed x3 -> x0, matrix products: 6.53 us -> none
    reduce_sum x9 -> x0, other arithmetic: 3.85 us -> none  [the longest x3 1.14 us: attend(): jnp.sum(cache_exp, axis=-1, keepdims=True)]
    another operation x8 -> x0, other arithmetic: 3.38 us -> none
  transfers between devices with their start and end apart: 10 -> 0, of which waited for: 7 -> 0; matrix products, arithmetic and copies ran while one was open for 20% -> 0% of each run, Pallas kernels for 0% -> 0%
where the time goes in v1:
time: 108 us
  Pallas kernels  108 us (100%)
    pallas_call x1, Pallas kernels, local(): pl.pallas_call(project, out_shape=(jax.ShapeDtypeStruct((REQS * QROWS, 12...  96.3 us
    pallas_call x1, Pallas kernels, local(): pl.pallas_call(attend, out_shape=jax.ShapeDtypeStruct((STEPS, REQS, 1024)...  11.6 us

profile of v1, /device:TPU:0, one launch (start us, length us, event | category | flops | bytes accessed | tf_op | source)
XLA Modules:
  0.0 107.9 jit_solution(4618243717411768218)
XLA Ops:
  0.0 96.3 %shard_map.91 = (f32[3072,128]{1,0:T(8,128)}, f32[1024,128]{1,0:T(8,128)}, f32[1024,128]{1,0:T(8,128)}) custom-call(bf16[384,1024]{1,0:T(8,128)(2,1)} %bitcast.16, bf16[8192,1280]{1,0:T(8,128)(2,1)} %bitcast.11, bf16[512,1024]{1,0:T(8,128)(2,1)} %bitcast.15, bf16[512,1280]{1,0:T(8,128)(2,1)} %bitcast.14, s32[1,128]{1,0:T(1,128)} %bitcast.18, ...), custom_call_target="tpu_custom_call" | custom-call | tf_op jit(solution)/shard_map/pallas_call | solution.py:513
  96.3 11.6 %shard_map.92 = bf16[3,128,1024]{2,1,0:T(8,128)(2,1)} custom-call(s32[128]{0:T(128)} %lens.1, f32[3072,128]{1,0:T(8,128)} %get-tuple-element.8.query, f32[1024,128]{1,0:T(8,128)} %get-tuple-element.9.key, f32[1024,128]{1,0:T(8,128)} %get-tuple-element.10.value, bf16[128,128,128]{2,1,0:T(8,128)(2,1)} %bitcast.12, bf16[128,128,128]{2,1,0:T(8,128)(2,1)} %bitcast.13), custom_call_target="tpu_custom_call" | custom-call | tf_op jit(solution)/shard_map/pallas_call | solution.py:563

commit v2 on v1

v2 whole, which is shorter than its diff:
```python
import functools

import jax
import jax.numpy as jnp
import numpy as np
from jax import lax
from jax.experimental import pallas as pl
from jax.experimental.pallas import tpu as pltpu
from jax.sharding import PartitionSpec as P

MESH = pl.DeviceIdType.MESH
F32 = jnp.float32
BF16 = jnp.bfloat16
STEPS = 3
REQS = 128
ROWS = STEPS * REQS
WIDTH = 1024
OUT = 1280
RANKS = 512
UP_PARTS = 4
UP_ROWS = RANKS // UP_PARTS
BLOCK = 32
BLOCKS = REQS // BLOCK
BROWS = STEPS * BLOCK
HALF = BROWS // 2
SUB = 16
PACK = ROWS // 2
PART = PACK // 8
PARTPAD = 32
QROWS = 24


def dot(a, b):
    return jnp.dot(a, b, preferred_element_type=F32)


def dot_nt(a, b):
    return lax.dot_general(a, b, (((1,), (1,)), ((), ())), preferred_element_type=F32)


def column(row):
    return jnp.transpose(jnp.broadcast_to(row, (128, 128)))


def verify(
    hid,
    weight,
    down,
    up,
    keys_in,
    values_in,
    req_ref,
    table_ref,
    len_ref,
    out,
    xs,
    rows,
    draw,
    wt,
    ups,
    wbuf,
    base,
    hits,
    spread,
    acc,
    reqs,
    slots,
    lengths,
    cosine,
    sine,
    home,
    home_in,
    part_in,
    low_part,
    low_parts,
    low_own,
    lows,
    low_both,
    dsend,
    relay_in,
    back_in,
    keys,
    values,
    query,
    new_key,
    new_value,
    mixed,
    ssem,
    rsem,
    lsem,
):
    rep = lax.axis_index("rep")
    tp = lax.axis_index("tp")
    x, z, y, c = rep // 4, rep % 4, tp // 2, tp % 2
    r = z * (1 - c) + x * c
    w = x * (1 - c) + z * c

    def rep_at(r_, w_):
        return (w_ * (1 - c) + r_ * c) * 4 + r_ * (1 - c) + w_ * c

    def dev(rep_, tp_):
        return {"rep": rep_, "tp": tp_}

    shift = (0, 3, 1, 2)
    row_reps = [rep_at((r + s) % 4, w) for s in shift]
    weight_reps = [rep_at(r, (w + s) % 4) for s in shift]
    row_dev = [dev(q, tp) for q in row_reps]
    weight_dev = [dev(q, tp) for q in weight_reps]
    tps = [((y + s) % 4) * 2 + c for s in shift]
    sib_tps = [((y + s) % 4) * 2 + 1 - c for s in shift]
    y_dev = [dev(rep, q) for q in tps]
    sibling = dev(rep, sib_tps[0])
    tp_dev = [dev(rep, (tp + k) % 8) for k in range(8)]

    count = [0]

    def remote(src, dst, device):
        i = count[0]
        count[0] += 1
        return pltpu.make_async_remote_copy(
            src_ref=src,
            dst_ref=dst,
            send_sem=ssem.at[i],
            recv_sem=rsem.at[i],
            device_id=device,
            device_id_type=MESH,
        )

    lcount = [0]

    def local(src, dst):
        i = lcount[0]
        lcount[0] += 1
        return pltpu.make_async_copy(src, dst, lsem.at[i])

    sent = []

    def go(*copies):
        for cp in copies:
            cp.start()
            sent.append(cp)

    class Ring:
        def __init__(self, src, slot, size, devs):
            a, b = (pl.ds(0, size // 2), pl.ds(size // 2, size // 2)) if size else (0, 1)
            left, right = devs[1], devs[2]
            self.first = [
                remote(src(a), slot(1, a), right),
                remote(src(b), slot(2, b), left),
            ]
            self.second = [
                remote(src(b), slot(1, b), right),
                remote(src(a), slot(2, a), left),
            ]
            self.far = [
                remote(slot(1, a), slot(3, a), right),
                remote(slot(2, b), slot(3, b), left),
            ]

        def relay(self):
            for i in range(2):
                self.first[i].wait_recv()
                go(self.far[i])

        def near(self):
            for i in range(2):
                self.second[i].wait_recv()

        def rest(self):
            for i in range(2):
                self.far[i].wait_recv()

    load_rows = local(hid, rows.at[0])
    load_down = local(down, draw)
    load_up = local(up, ups.at[0])
    order = ((0, 0), (0, 1), (1, 0), (2, 0), (1, 1), (2, 1), (3, 0), (3, 1))
    load_w = []
    for n, (i, s) in enumerate(order):
        t_ = (tps if s == 0 else sib_tps)[i]
        load_w.append(
            local(weight.at[pl.ds(pl.multiple_of(t_ * WIDTH, WIDTH), WIDTH), :], wbuf.at[n % 4])
        )
    load_keys = local(keys_in, keys)
    load_values = local(values_in, values)
    load_down.start()
    load_rows.start()
    load_w[0].start()
    load_w[1].start()

    reqs[0] = jnp.broadcast_to(req_ref[...], (8, 128))

    barrier = pltpu.get_barrier_semaphore()
    peers = [row_dev[1], row_dev[2], row_dev[3], weight_dev[1], weight_dev[2]] + tp_dev[1:]
    for peer in peers:
        pl.semaphore_signal(barrier, inc=1, device_id=peer, device_id_type=MESH)
    load_down.wait()
    for h in range(2):
        wt[0, h] = jnp.transpose(draw[h * 256 : (h + 1) * 256, :])
    pl.semaphore_wait(barrier, len(peers))

    y_ring = Ring(lambda h: hid.at[h], lambda s, h: xs.at[2 * s - 1, h], ROWS, y_dev)
    r_ring = Ring(lambda h: hid.at[h], lambda s, h: rows.at[s, h], ROWS, row_dev)
    w_ring = Ring(lambda h: wt.at[0, h], lambda s, h: wt.at[s, h], 0, weight_dev)
    up_rings = []
    for k in range(UP_PARTS):
        part = pl.ds(k * UP_ROWS, UP_ROWS)
        up_rings.append(
            Ring(
                lambda h, part=part: up.at[part, :].at[h],
                lambda s, h, part=part: ups.at[s, part, :].at[h],
                UP_ROWS,
                weight_dev,
            )
        )
    req_copies = [remote(reqs.at[0], reqs.at[(0, 2, 1, 3)[i]], row_dev[i]) for i in (1, 2, 3)]
    sib_copies = [remote(hid, xs.at[0], sibling)] + [
        remote(xs.at[2 * i - 1], xs.at[2 * i], sibling) for i in (1, 2, 3)
    ]

    go(*req_copies)
    go(*w_ring.first, *r_ring.first, *y_ring.first)
    go(*w_ring.second, *r_ring.second, *y_ring.second)
    go(sib_copies[0])
    load_w[2].start()
    load_w[3].start()
    load_up.start()
    load_keys.start()
    load_values.start()

    lane = lax.broadcasted_iota(jnp.int32, (128, 128), 1)
    low_lane = lane < 64

    freq = jnp.exp((lane % 64).astype(F32) * (-2.0 / 128) * jnp.log(F32(500000.0)))
    lengths[...] = column(len_ref[...])
    pos = lengths[...].astype(F32)
    for t in range(STEPS):
        angle = (pos + t) * freq
        part = pl.ds(t * REQS, REQS)
        cosine[part, :] = jnp.cos(angle)
        sine[part, :] = jnp.where(low_lane, -1.0, 1.0) * jnp.sin(angle)

    def rotate(v, at):
        return v * cosine[at, :] + pltpu.roll(v, 64, 1) * sine[at, :]

    def find_slots(i):
        hit = column(reqs[i, 0:1, :]) == lane
        found = jnp.sum(
            jnp.where(hit, jnp.broadcast_to(table_ref[...], (128, 128)), 0).astype(F32),
            axis=1,
            keepdims=True,
        )
        slots[i] = jnp.broadcast_to(found, (128, 128)).astype(jnp.int32)
        for j in range(4):
            for p in range(4):
                target = weight_reps[j] * 8 + 2 * p + jnp.where(low_lane, 0, 1)
                at = (j * 4 + p) * 128
                hits[i, :, at : at + 128] = jnp.where(slots[i] == target, 1.0, 0.0).astype(BF16)

    find_slots(0)

    done = [0]

    def base_mm(x_ref):
        n = done[0]
        done[0] += 1
        load_w[n].wait()
        got = dot(x_ref[...], wbuf[n % 4])
        if n == 0:
            base[...] = got
        else:
            base[...] += got
        if n + 4 < 8:
            load_w[n + 4].start()

    def down_mm(i, j, n=1):
        @pl.loop(0, 2)
        def _(h):
            got = dot(rows[i : i + n].reshape(n * ROWS, WIDTH), wt[j, h])
            for p in range(2):
                target = weight_reps[j] * 8 + h * 4 + 2 * p + jnp.where(low_lane, 0, 1)
                for q in range(n):
                    hit = slots[i + q] == target
                    for t in range(STEPS):
                        at = q * ROWS + t * REQS
                        acc[i + q, pl.ds(t * REQS, REQS), :] += jnp.where(
                            hit, got[at : at + REQS, p * 128 : (p + 1) * 128], 0.0
                        )

    acc[...] = jnp.zeros_like(acc)
    load_rows.wait()
    base_mm(rows.at[0])
    down_mm(0, 0)
    for cp in req_copies:
        cp.wait_recv()
    for i in (1, 2, 3):
        find_slots(i)
    sib_copies[0].wait_recv()
    base_mm(xs.at[0])

    y_ring.relay()
    r_ring.relay()
    w_ring.relay()
    for ring in up_rings:
        go(*ring.first, *ring.second)

    y_ring.near()
    go(sib_copies[1], sib_copies[2])
    r_ring.near()
    down_mm(1, 0, 2)
    base_mm(xs.at[1])
    w_ring.near()
    down_mm(0, 1, 3)
    down_mm(0, 2, 3)
    base_mm(xs.at[3])
    y_ring.rest()
    go(sib_copies[3])
    r_ring.rest()
    for j in (0, 1, 2):
        down_mm(3, j)
    w_ring.rest()

    home_copies = []
    lane_h = lax.broadcasted_iota(jnp.int32, (PACK, 128), 1) < 64
    for i in (3, 1, 2, 0):
        down_mm(i, 3)
        both = acc[i] + pltpu.roll(acc[i], 64, 1)
        home[i] = jnp.where(lane_h, both[:PACK], both[PACK:])
        if i:
            cp = remote(home.at[i], home_in.at[(0, 2, 1, 3)[i]], row_dev[i])
            home_copies.append(cp)
            go(cp)
    up_rings[0].relay()
    sib_copies[1].wait_recv()
    base_mm(xs.at[2])
    for cp in home_copies:
        cp.wait_recv()
    home[0] = (home[0] + home_in[1]) + (home_in[2] + home_in[3])
    part_copies = []
    for k in range(1, 8):
        target = (tp + k) % 8
        cp = remote(
            home.at[0, pl.ds(pl.multiple_of(target * PART, 8), PART), :], part_in.at[k], tp_dev[k]
        )
        part_copies.append(cp)
        go(cp)
    up_rings[1].relay()
    sib_copies[2].wait_recv()
    base_mm(xs.at[4])
    for cp in part_copies:
        cp.wait_recv()
    total = home[0, pl.ds(pl.multiple_of(tp * PART, 8), PART), :]
    for k in range(1, 8):
        total = total + part_in[k]
    low_part[...] = jnp.concatenate([total, jnp.zeros((PARTPAD - PART, 128), F32)], 0).astype(BF16)
    low_copies = []
    for k in range(1, 8):
        cp = remote(low_part, low_parts.at[k], tp_dev[k])
        low_copies.append(cp)
        go(cp)
    up_rings[2].relay()
    base_mm(xs.at[5])
    for cp in low_copies:
        cp.wait_recv()
    low_own[pl.ds(pl.multiple_of(tp * PART, 8), PART), :] = low_part[...].astype(F32)[:PART]
    for k in range(1, 8):
        source = (tp + 8 - k) % 8
        low_own[pl.ds(pl.multiple_of(source * PART, 8), PART), :] = low_parts[k].astype(F32)[:PART]
    lows[0] = low_own[...].astype(BF16)
    back_low = [remote(lows.at[0], lows.at[(0, 2, 1, 3)[i]], row_dev[i]) for i in (1, 2, 3)]
    go(*back_low)

    def unpack(i):
        packed = lows[i].astype(F32)
        turned = pltpu.roll(packed, 64, 1)
        low_both[i, :PACK, :] = jnp.where(lane_h, packed, turned).astype(BF16)
        low_both[i, PACK:, :] = jnp.where(lane_h, turned, packed).astype(BF16)

    unpack(0)
    up_rings[3].relay()
    sib_copies[3].wait_recv()
    base_mm(xs.at[6])
    for cp in back_low:
        cp.wait_recv()
    for i in (1, 2, 3):
        unpack(i)
    load_up.wait()
    for ring in up_rings:
        ring.near()
        ring.rest()

    ha, hb = pl.ds(0, HALF), pl.ds(HALF, HALF)
    far_back, near_back, late_back = {}, {}, {}

    def send_block(b):
        for i in range(4):
            for t in range(STEPS):
                low = low_both[i, t * REQS + b * BLOCK : t * REQS + (b + 1) * BLOCK, :]
                at = i * BROWS + t * BLOCK
                for n in range(16):
                    spread[at : at + BLOCK, n * 128 : (n + 1) * 128] = (
                        hits[i, b * BLOCK : (b + 1) * BLOCK, n * 128 : (n + 1) * 128] * low
                    )
        got = dot(spread[...], ups[...].reshape(4 * RANKS, OUT)).astype(BF16)
        for i in range(4):
            dsend[b, i] = got[i * BROWS : (i + 1) * BROWS]
        far_back[b] = [
            remote(dsend.at[b, 3, ha], relay_in.at[0, b], row_dev[2]),
            remote(dsend.at[b, 3, hb], relay_in.at[1, b], row_dev[1]),
        ]
        near_back[b] = [
            remote(dsend.at[b, 2, hb], back_in.at[0, b, hb], row_dev[2]),
            remote(dsend.at[b, 1, ha], back_in.at[1, b, ha], row_dev[1]),
        ]
        go(*far_back[b], *near_back[b])

    def relay_block(b):
        far_back[b][0].wait_recv()
        dsend[b, 2, ha, :] = dsend[b, 2, ha, :] + relay_in[0, b]
        far_back[b][1].wait_recv()
        dsend[b, 1, hb, :] = dsend[b, 1, hb, :] + relay_in[1, b]
        late_back[b] = [
            remote(dsend.at[b, 2, ha], back_in.at[0, b, ha], row_dev[2]),
            remote(dsend.at[b, 1, hb], back_in.at[1, b, hb], row_dev[1]),
        ]
        go(*late_back[b])

    factor = 128**-0.5

    def attend(b, s):
        first = b * BLOCK + s * SUB
        n_rows = SUB * QROWS
        q = query[pl.ds(pl.multiple_of(s * n_rows, 8), n_rows), :].astype(BF16)
        fresh_at = pl.ds(pl.multiple_of(s * SUB * 8, 8), SUB * 8)
        row = lax.broadcasted_iota(jnp.int32, (n_rows, 128), 0)
        col = lax.broadcasted_iota(jnp.int32, (n_rows, 128), 1)
        open_ = (row // QROWS == col // 8) & (col % 8 <= (row % QROWS) // 8)
        fresh = dot_nt(q, new_key[fresh_at, :].astype(BF16)) * factor
        fresh = jnp.where(open_, fresh, -jnp.inf)
        lane_q = lax.broadcasted_iota(jnp.int32, (QROWS, 128), 1)
        parts = []
        for i in range(SUB // 2):
            pair = keys[pl.ds(first + 2 * i, 2)].reshape(256, 128)
            got = dot_nt(q[2 * i * QROWS : (2 * i + 2) * QROWS], pair) * factor
            for k in range(2):
                length = jnp.broadcast_to(lengths[pl.ds(first + 2 * i + k, 1), :], (QROWS, 128))
                parts.append(
                    jnp.where(
                        lane_q < length,
                        got[k * QROWS : (k + 1) * QROWS, k * 128 : (k + 1) * 128],
                        -jnp.inf,
                    )
                )
        cached = jnp.concatenate(parts, 0)
        highest = jnp.max(jnp.maximum(cached, fresh), axis=1, keepdims=True)
        cached = jnp.exp(cached - highest)
        fresh = jnp.exp(fresh - highest)
        scale = 1.0 / jnp.sum(cached + fresh, axis=1, keepdims=True)
        cached = (cached * scale).astype(BF16)
        fresh = (fresh * scale).astype(BF16)
        extra = dot(fresh, new_value[fresh_at, :].astype(BF16))
        for i in range(SUB):
            at = i * QROWS
            mixed[at : at + QROWS, :] = extra[at : at + QROWS] + dot(
                cached[at : at + QROWS], values[first + i]
            )
        for t in range(STEPS):
            for g in range(8):
                out[t, pl.ds(pl.multiple_of(first, SUB), SUB), g * 128 : (g + 1) * 128] = mixed[
                    pl.ds(t * 8 + g, SUB, stride=QROWS), :
                ].astype(BF16)

    def finish_block(b):
        for cp in near_back[b] + late_back[b]:
            cp.wait_recv()
        for t in range(STEPS):
            at = slice(t * BLOCK, (t + 1) * BLOCK)
            whole = slice(t * REQS + b * BLOCK, t * REQS + (b + 1) * BLOCK)
            add = (dsend[b, 0, at, :].astype(F32) + back_in[0, b, at, :].astype(F32)) + back_in[
                1, b, at, :
            ].astype(F32)
            joined = base[whole, :] + add
            for g in range(8):
                query[pl.ds(t * 8 + g, BLOCK, stride=QROWS), :] = rotate(
                    joined[:, g * 128 : (g + 1) * 128], whole
                )
            new_key[pl.ds(t, BLOCK, stride=8), :] = rotate(joined[:, 1024:1152], whole)
            new_value[pl.ds(t, BLOCK, stride=8), :] = joined[:, 1152:]

        @pl.loop(0, BLOCK // SUB)
        def _(s):
            attend(b, s)

    new_key[...] = jnp.zeros_like(new_key)
    new_value[...] = jnp.zeros_like(new_value)
    send_block(0)
    send_block(1)
    relay_block(0)
    send_block(2)
    relay_block(1)
    send_block(3)
    relay_block(2)
    load_keys.wait()
    load_values.wait()
    finish_block(0)
    relay_block(3)
    finish_block(1)
    finish_block(2)
    finish_block(3)
    for cp in sent:
        cp.wait_send()


def local(
    normed_hidden_input,
    query_key_value_weight,
    adapter_down_weight,
    adapter_up_weight,
    cached_rotated_keys,
    cached_value_rows,
    cached_length_valid,
    request_adapter,
    adapter_storage_slot,
):
    hid = normed_hidden_input.reshape(ROWS, WIDTH)
    weight = query_key_value_weight.reshape(8 * WIDTH, OUT)
    down = jnp.swapaxes(adapter_down_weight, 1, 2).reshape(RANKS, WIDTH)
    up = adapter_up_weight.reshape(RANKS, OUT)
    anywhere = pl.BlockSpec(memory_space=pl.ANY)
    in_vmem = pl.BlockSpec(memory_space=pltpu.VMEM)
    copies = 140
    return pl.pallas_call(
        verify,
        out_shape=jax.ShapeDtypeStruct((STEPS, REQS, 1024), BF16),
        in_specs=[anywhere] * 6 + [in_vmem] * 3,
        out_specs=in_vmem,
        scratch_shapes=[
            pltpu.VMEM((7, ROWS, WIDTH), BF16),
            pltpu.VMEM((4, ROWS, WIDTH), BF16),
            pltpu.VMEM((RANKS, WIDTH), BF16),
            pltpu.VMEM((4, 2, WIDTH, 256), BF16),
            pltpu.VMEM((4, RANKS, OUT), BF16),
            pltpu.VMEM((4, WIDTH, OUT), BF16),
            pltpu.VMEM((ROWS, OUT), F32),
            pltpu.VMEM((4, REQS, 4 * RANKS), BF16),
            pltpu.VMEM((4 * BROWS, 4 * RANKS), BF16),
            pltpu.VMEM((4, ROWS, 128), F32),
            pltpu.VMEM((4, 8, 128), jnp.int32),
            pltpu.VMEM((4, 128, 128), jnp.int32),
            pltpu.VMEM((REQS, 128), jnp.int32),
            pltpu.VMEM((ROWS, 128), F32),
            pltpu.VMEM((ROWS, 128), F32),
            pltpu.VMEM((4, PACK, 128), F32),
            pltpu.VMEM((4, PACK, 128), F32),
            pltpu.VMEM((8, PART, 128), F32),
            pltpu.VMEM((PARTPAD, 128), BF16),
            pltpu.VMEM((8, PARTPAD, 128), BF16),
            pltpu.VMEM((PACK, 128), F32),
            pltpu.VMEM((4, PACK, 128), BF16),
            pltpu.VMEM((4, ROWS, 128), BF16),
            pltpu.VMEM((BLOCKS, 4, BROWS, OUT), BF16),
            pltpu.VMEM((2, BLOCKS, HALF, OUT), BF16),
            pltpu.VMEM((2, BLOCKS, BROWS, OUT), BF16),
            pltpu.VMEM((REQS, 128, 128), BF16),
            pltpu.VMEM((REQS, 128, 128), BF16),
            pltpu.VMEM((BLOCK * QROWS, 128), F32),
            pltpu.VMEM((BLOCK * 8, 128), F32),
            pltpu.VMEM((BLOCK * 8, 128), F32),
            pltpu.VMEM((SUB * QROWS, 128), F32),
            pltpu.SemaphoreType.DMA((copies,)),
            pltpu.SemaphoreType.DMA((copies,)),
            pltpu.SemaphoreType.DMA((16,)),
        ],
        compiler_params=pltpu.CompilerParams(
            collective_id=0, has_side_effects=True, vmem_limit_bytes=62 << 20
        ),
    )(
        hid,
        weight,
        down,
        up,
        cached_rotated_keys.reshape(REQS, 128, 128),
        cached_value_rows.reshape(REQS, 128, 128),
        request_adapter.reshape(1, REQS),
        adapter_storage_slot.reshape(1, 128),
        cached_length_valid.reshape(1, REQS),
    )


def solution(mesh):
    placed = (
        P(None, "rep", "tp"),
        P(None, "tp", None),
        P("rep", "tp", None),
        P("rep", None, "tp", None),
        P("rep", "tp", None, None),
        P("rep", "tp", None, None),
        P("rep"),
        P("rep"),
        P(),
    )
    return jax.shard_map(
        local, mesh=mesh, in_specs=placed, out_specs=P(None, "rep", "tp"), check_vma=False
    )
```

time: 108 us -> 94.3 us (0.87)
  Pallas kernels: 108 us -> 92.1 us
  local copies, waits for them, and re-layouts: 0 us -> 2.06 us
    pallas_call x2 -> x1, Pallas kernels: 108 us -> 92.1 us  [local(): pl.pallas_call(verify, out_shape=jax.ShapeDtypeStruct((STEPS, REQS, 1024)...]
    unnamed x0 -> x1, local copies, waits for them, and re-layouts: none -> 2.06 us
where the time goes in v2:
time: 94.3 us; the launch traced here: 94.2 us
  Pallas kernels  92.1 us (98%)
  local copies, waits for them, and re-layouts  2.06 us (2%)
    pallas_call x1, Pallas kernels, local(): pl.pallas_call(verify, out_shape=jax.ShapeDtypeStruct((STEPS, REQS, 1024)...  92.1 us
    unnamed x1, local copies, waits for them, and re-layouts  2.06 us

profile of v2, /device:TPU:0, one launch (start us, length us, event | category | flops | bytes accessed | tf_op | source)
XLA Modules:
  0.0 94.2 jit_solution(11104282995664738755)
XLA Ops:
  0.0 92.1 %shard_map.91 = bf16[3,128,1024]{2,1,0:T(8,128)(2,1)} custom-call(bf16[384,1024]{1,0:T(8,128)(2,1)} %bitcast.16, bf16[8192,1280]{1,0:T(8,128)(2,1)} %bitcast.11, bf16[512,1024]{1,0:T(8,128)(2,1)} %bitcast.15, bf16[512,1280]{1,0:T(8,128)(2,1)} %bitcast.14, bf16[128,128,128]{2,1,0:T(8,128)(2,1)} %bitcast.12, bf16[128,128,128]{2,1,0:T(8,128)(2,1)} %bitcast.13, ...), custom_call_target="tpu_custom_call" | custom-call | tf_op jit(solution)/shard_map/pallas_call | solution.py:531
  92.1 2.1 %copy.11 = bf16[3,128,1024]{2,1,0:T(8,128)(2,1)} copy(bf16[3,128,1024]{2,1,0:T(8,128)(2,1)} %shard_map.91) | data formatting | bytes 1572864
